TPU v7x, 32 devices: a whole 2x2x4 slice. The times are simulated.
32 devices in a mesh: space: 8 (over z, core), chaos: 4 (over y, x).
Axes of the slice: x: 2, y: 2, z: 4, core: 2. Of those that a mesh axis runs over, the one named last changes fastest.
Arguments:
- chaos_modes: float32 [84, 32768], P(None, ('space', 'chaos')), may hold values from -0.2 to 0.2
- newton_heading: float32 [84, 32768], P(None, ('space', 'chaos')), may hold values from -0.2 to 0.2
- source: float32 [32768], P(('space', 'chaos')), may hold values from -6 to 6
- nodes: float32 [512, 6], replicated, may hold values from -3 to 3
- weights: float32 [512], replicated, may hold values from 0.0009765625 to 0.0029296875
- k_ref: float32 [4], replicated, may hold values from 0.5 to 4
- sensitivity: float32 [4, 6], replicated, may hold values from -0.1 to 0.1
- decay: float32 [4], replicated, may hold values from 0.1 to 0.5
- material: int32 [512], P('space'), may hold values from 0 to 3
- neighbors: int32 [512, 4], P('space'), may hold values from -1 to 79, as said below
- send_list: int32 [8, 8, 2], P('space'), may hold values from 0 to 63, as said below
Outputs:
- residual: float32 [84, 32768], P(None, ('space', 'chaos'))
- jvp_out: float32 [84, 32768], P(None, ('space', 'chaos'))
Inputs may be any that keep to these rules, and one draw needn't show every extreme that they name: `neighbors`: -1 marks a face without neighbour. An entry below 64 is a block of the same partition; an entry 64 + t * 2 + j names slot j of what partition t sends here, where t is one or two indices away along space, cyclically, and the slot is live. send_list[s, t, j] is a local block of partition s. Only slots named by some neighbour entry are live: from s to a partition one or two indices away, cyclically, between 1 and 2 leading slots; to any other partition none.
All inputs are finite; a program needn't handle non-finite values.
Results may differ from a plain program's by a relative error of at most 0.0003.
Values sent between devices are 32-bit elements; how exact they have to be, the bound alone decides.
A program may use at most 192 MiB of HBM per device.

v0:
```python
import functools
import math

import jax
import jax.numpy as jnp
import numpy as np
from jax import lax
from jax.experimental import pallas as pl
from jax.experimental.pallas import tpu as pltpu
from jax.sharding import PartitionSpec as P

NMAT = 4
SITES = 64
TERMS = 84
MAIN = 80
LOG2E = 1.0 / math.log(2.0)
LN2 = math.log(2.0)
OFFSETS = (1, -1, 2, -2)
BF = jnp.bfloat16
F32 = jnp.float32


def compositions(remaining, places):
    if places == 1:
        return [[remaining]]
    listing = []
    for leading in range(remaining, -1, -1):
        for trailing in compositions(remaining - leading, places - 1):
            listing.append([leading] + trailing)
    return listing


def chaos_orders(variables):
    listing = []
    for degree in range(4):
        listing = listing + compositions(degree, variables)
    return np.array(listing, dtype=np.int32)


def half_turn(x, wanted):
    return jnp.where(wanted, pltpu.roll(x, 64, 1), x)


def factors(x, o):
    second = (x * x - 1.0) * np.float32(1.0 / math.sqrt(2.0))
    third = (x * x * x - 3.0 * x) * np.float32(1.0 / math.sqrt(6.0))
    return jnp.where(o == 0, 1.0, jnp.where(o == 1, x, jnp.where(o == 2, second, third)))


def order_codes(dims):
    orders = chaos_orders(dims)
    code = (orders * 4 ** np.arange(dims)[None, :]).sum(1)
    rest = np.arange(MAIN, TERMS)
    first = np.arange(MAIN)
    column = np.concatenate([first, first, first, rest, rest, rest, np.zeros(4, np.int64)])
    out = np.zeros((8, 256), np.float32)
    out[0] = code[column]
    out[1, :TERMS] = code
    return out


def upright(row):
    return jnp.transpose(jnp.broadcast_to(row, (128, 128)))


def fill_tables(nodes_t, weights, codes, left, right, mass):
    dims = nodes_t.shape[0]
    column = lax.broadcasted_iota(jnp.int32, (1, 128), 1)
    code_right = upright(codes[1:2, 0:128])[0:88].astype(jnp.int32)
    row = lax.broadcasted_iota(jnp.int32, (88, 1), 0)
    mass[...] = jnp.zeros(mass.shape, F32)

    def body(part, carry):
        span = pl.ds(pl.multiple_of(part * 128, 128), 128)
        points = [nodes_t[d : d + 1, span] for d in range(dims)]
        stood = [upright(x) for x in points]
        for side in range(2):
            code = codes[0:1, side * 128 : side * 128 + 128].astype(jnp.int32)
            at = column + side * 128
            lower = ((at >= 160) & (at < 240)) | ((at >= 248) & (at < 252))
            value = None
            for d in range(dims):
                f = factors(stood[d], (code // 4**d) % 4)
                value = f if value is None else value * f
            high = value.astype(BF).astype(F32)
            value = jnp.where(lower, value - high, high)
            left[span, side * 128 : side * 128 + 128] = jnp.where(at < 252, value, 0.0).astype(BF)
        value = weights[:, span]
        for d in range(dims):
            value = value * factors(points[d], (code_right // 4**d) % 4)
        value = jnp.where(row < TERMS, value, 0.0)
        high = value.astype(BF).astype(F32)
        right[:, span] = jnp.concatenate([high, value - high], 0).astype(BF)
        mass[...] += jnp.sum(value, axis=1, keepdims=True)
        return carry

    lax.fori_loop(0, nodes_t.shape[1] // 128, body, 0)


def fill_aux(k_ref, sensitivity, decay, material, table, field):
    row = lax.broadcasted_iota(jnp.int32, (8, 128), 0)
    low_half = lax.broadcasted_iota(jnp.int32, (8, 128), 1) < 64
    dims = sensitivity.shape[1]
    for m in range(NMAT):
        tile = jnp.log(jnp.full((8, 128), k_ref[m], F32))
        for d in range(dims):
            tile = jnp.where(row == d + 1, sensitivity[m, d], tile)
        tile = jnp.where(row == 7, -decay[m], tile)
        table[m] = tile * np.float32(LOG2E)
    for i in range(material.shape[0] // 2):
        field[i, 168:176] = jnp.where(low_half, table[material[2 * i]], table[material[2 * i + 1]])


def remote(src, dst, send, recv, device):
    return pltpu.make_async_remote_copy(
        src_ref=src, dst_ref=dst, send_sem=send, recv_sem=recv,
        device_id=device, device_id_type=pl.DeviceIdType.MESH,
    )


def pack_own(modes, heading, pairs, base, field):
    for i in range(pairs):
        cols = slice(i * 128, i * 128 + 128)
        field[base + i, 0:80] = modes[0:80, cols]
        field[base + i, 80:160] = heading[0:80, cols]
        field[base + i, 160:168] = jnp.concatenate([modes[80:84, cols], heading[80:84, cols]], 0)


def greet(space_count, chaos_count, space, chaos):
    barrier = pltpu.get_barrier_semaphore()
    if chaos_count == 4:
        peers = [chaos + 1 - 2 * (chaos % 2), (chaos + 2) % 4]
    else:
        peers = [(chaos + k) % chaos_count for k in range(1, chaos_count)]
    for peer in peers:
        pl.semaphore_signal(
            barrier, inc=1, device_id={"chaos": peer}, device_id_type=pl.DeviceIdType.MESH
        )
    for offset in OFFSETS:
        pl.semaphore_signal(
            barrier, inc=1, device_id={"space": (space + offset + space_count) % space_count},
            device_id_type=pl.DeviceIdType.MESH,
        )
    return barrier, peers


def spread_modes(chaos_count, peers, chaos, pairs, field, send, recv, meanwhile, early):
    def block(owner, first, count):
        return field.at[pl.ds(owner * pairs + first, count), 0:168]

    if chaos_count == 4:
        across, along = peers
        half = pairs // 2
        plan = [
            (chaos, 0, across), (chaos, half, along),
            (chaos, half, across), (chaos, 0, along),
        ]
        copies = [
            remote(block(o, f, half), block(o, f, half), send.at[i], recv.at[i], {"chaos": t})
            for i, (o, f, t) in enumerate(plan)
        ]
        for copy in copies:
            copy.start()
        meanwhile()
        copies[0].wait_recv()
        on = remote(
            block(across, 0, half), block(across, 0, half), send.at[4], recv.at[4],
            {"chaos": along},
        )
        on.start()
        copies[1].wait_recv()
        over = remote(
            block(along, half, half), block(along, half, half), send.at[5], recv.at[5],
            {"chaos": across},
        )
        over.start()
        early()
        copies[2].wait_recv()
        copies[3].wait_recv()
        on.wait_recv()
        over.wait_recv()
        return copies + [on, over]
    copies = [
        remote(
            block(chaos, 0, pairs), block(chaos, 0, pairs), send.at[i], recv.at[i], {"chaos": t}
        )
        for i, t in enumerate(peers)
    ]
    for copy in copies:
        copy.start()
    meanwhile()
    early()
    for copy in copies:
        copy.wait_recv()
    return copies


def send_halo(space_count, space, picks, field, out, inbox, send, recv):
    low_half = lax.broadcasted_iota(jnp.int32, (1, 128), 1) < 64
    copies = []
    for i, offset in enumerate(OFFSETS):
        target = (space + offset + space_count) % space_count
        e0 = picks[2 * target]
        e1 = picks[2 * target + 1]
        x0 = half_turn(field[e0 // 2], e0 % 2 == 1)
        x1 = half_turn(field[e1 // 2], e1 % 2 == 0)
        out[i] = jnp.where(low_half, x0, x1)
        copy = remote(out.at[i], inbox.at[i], send.at[i], recv.at[i], {"space": target})
        copy.start()
        copies.append(copy)
    return copies


def whole_kernel(
    sizes, picks, k_ref, sensitivity, decay, material, neighbors, modes_far, heading_far,
    nodes_far, weights_far, codes_far, source, res, jvp,
    field, left, right, mass, rhs, kc, acc,
    modes, heading, nodes_t, weights, codes, table, out, inbox,
    send, recv, halo_send, halo_recv, near,
):
    space_count, chaos_count, pairs, halo_depth = sizes
    space = lax.axis_index("space")
    chaos = lax.axis_index("chaos")
    blocks = material.shape[0]
    barrier, peers = greet(space_count, chaos_count, space, chaos)
    loads = [
        pltpu.make_async_copy(a, b, near.at[i])
        for i, (a, b) in enumerate(
            [
                (modes_far, modes), (heading_far, heading), (nodes_far, nodes_t),
                (weights_far, weights), (codes_far, codes),
            ]
        )
    ]
    for load in loads:
        load.start()
    fill_aux(k_ref, sensitivity, decay, material, table, field)
    for load in loads:
        load.wait()
    pack_own(modes, heading, pairs, chaos * pairs, field)
    pl.semaphore_wait(barrier, len(peers) + len(OFFSETS))
    base = chaos * pairs
    ranks = (space, space_count, blocks)

    def early():
        def body(pair, carry):
            pair_first(pair, base, field, left, rhs, kc, acc)
            return carry

        lax.fori_loop(0, pairs, body, 0)

    copies = spread_modes(
        chaos_count, peers, chaos, pairs, field, send, recv,
        lambda: fill_tables(nodes_t, weights, codes, left, right, mass),
        early,
    )
    halo = send_halo(space_count, space, picks, field, out, inbox, halo_send, halo_recv)
    for copy in copies:
        copy.wait_send()
    for i, copy in enumerate(halo):
        copy.wait()
        field[blocks // 2 + i] = inbox[i]

    def late(pair, carry):
        pair_second(
            pair, base, ranks, halo_depth, neighbors, field, left, right, mass, source, res,
            jvp, rhs, kc, acc,
        )
        return carry

    lax.fori_loop(0, pairs, late, 0)


def place_rhs(rhs, face, field, main, tail):
    cols = slice(field * 128, field * 128 + 128)
    row = lax.broadcasted_iota(jnp.int32, (8, 128), 0)
    high = main.astype(BF)
    low = (main - high.astype(F32)).astype(BF)
    tail_high = tail.astype(BF).astype(F32)
    rhs[face, 0:80, cols] = high
    rhs[face, 80:160, cols] = low
    rhs[face, 160:240, cols] = high
    rhs[face, 240:256, cols] = jnp.concatenate(
        [
            jnp.where(row < 4, tail_high, tail - tail_high),
            jnp.where(row < 4, tail_high, 0.0),
        ],
        0,
    ).astype(BF)


def fields(x):
    row = lax.broadcasted_iota(jnp.int32, (8, 128), 0)
    mixed = x[160:168]
    turned = pltpu.roll(mixed, 4, 0)
    mode = (x[0:80], jnp.where(row < 4, mixed, turned))
    step = (x[80:160], jnp.where(row < 4, turned, mixed))
    aux = x[168:176]
    damp = aux[7:8]
    offset = jnp.where(row < 7, aux, 0.0)
    arg_main = mode[0] * damp
    arg_main = jnp.concatenate([arg_main[0:8] + offset, arg_main[8:80]], 0)
    arg = (arg_main, mode[1] * damp)
    rate = damp * LN2
    change = (step[0] * rate, step[1] * rate)
    return mode, step, arg, change


def slot(neighbors, block, face, ranks, halo_depth):
    space, space_count, blocks = ranks
    entry = neighbors[face, block]
    away = jnp.maximum(entry - blocks, 0)
    distance = (space - away // halo_depth + space_count) % space_count
    order = jnp.where(
        distance == 1, 0, jnp.where(distance == space_count - 1, 1, jnp.where(distance == 2, 2, 3))
    )
    index = jnp.where(
        entry >= blocks, blocks + order * halo_depth + away % halo_depth, jnp.maximum(entry, 0)
    )
    return index, jnp.where(entry >= 0, np.float32(0.25), np.float32(0.0))


def face_sum(basis, rhs, face, conduct, change):
    r = jnp.dot(basis, rhs[face], preferred_element_type=F32)
    k = jnp.exp2(r[:, 256:384])
    a = conduct + k
    b = change + k * r[:, 384:512]
    gap = r[:, 0:128]
    return a * gap, b * gap + a * r[:, 128:256]


def place_face(rhs, face, gap, other):
    place_rhs(rhs, face, 0, *gap[0])
    place_rhs(rhs, face, 1, *gap[1])
    place_rhs(rhs, face, 2, *other[2])
    place_rhs(rhs, face, 3, *other[3])


def pair_first(pair, base, field, left, rhs, kc, acc):
    lane = lax.broadcasted_iota(jnp.int32, (1, 128), 1)
    height = lane % 64
    x = field[base + pair]
    mine = fields(x)
    place_rhs(rhs, 6, 0, *mine[2])
    place_rhs(rhs, 6, 1, *mine[3])
    for face in range(2):
        if face == 0:
            scale = jnp.where(height == 63, 0.0, 0.5)
            other = [tuple(pltpu.roll(a, 127, 1) for a in f) for f in mine]
            gap = [tuple((a - b) * scale for a, b in zip(mine[i], other[i])) for i in (0, 1)]
        else:
            scale = jnp.where(height == 0, 1.0, 0.5)
            bottom = height == 0
            other = [tuple(pltpu.roll(a, 1, 1) for a in f) for f in mine]
            gap = [
                tuple((a - jnp.where(bottom, 0.0, b)) * scale for a, b in zip(mine[i], other[i]))
                for i in (0, 1)
            ]
            other = [
                tuple(jnp.where(bottom, a, b) for a, b in zip(mine[i], other[i])) for i in range(4)
            ]
        place_face(rhs, face, gap, other)
    for part in range(left.shape[0] // 512):
        rows = slice(part * 512, part * 512 + 512)
        basis = left[rows]
        r = jnp.dot(basis, rhs[6, :, 0:256], preferred_element_type=F32)
        kc[pair, 0, rows] = jnp.exp2(r[:, 0:128])
        kc[pair, 1, rows] = kc[pair, 0, rows] * r[:, 128:256]
        for face in range(2):
            bal, step = face_sum(basis, rhs, face, kc[pair, 0, rows], kc[pair, 1, rows])
            if face == 0:
                acc[pair, 0, rows] = bal
                acc[pair, 1, rows] = step
            else:
                acc[pair, 0, rows] += bal
                acc[pair, 1, rows] += step


def pair_second(
    pair, base, ranks, halo_depth, neighbors, field, left, right, mass, source, res, jvp, rhs,
    kc, acc,
):
    lane = lax.broadcasted_iota(jnp.int32, (1, 128), 1)
    low_half = lane < 64
    mine = fields(field[base + pair])
    for face in range(2, 6):
        e0, c0 = slot(neighbors, 2 * (base + pair), face - 2, ranks, halo_depth)
        e1, c1 = slot(neighbors, 2 * (base + pair) + 1, face - 2, ranks, halo_depth)
        x0 = half_turn(field[e0 // 2], e0 % 2 == 1)
        x1 = half_turn(field[e1 // 2], e1 % 2 == 0)
        scale = jnp.where(low_half, c0, c1)
        other = fields(jnp.where(low_half, x0, x1))
        gap = [tuple((a - b) * scale for a, b in zip(mine[i], other[i])) for i in (0, 1)]
        place_face(rhs, face, gap, other)
    total = None
    for part in range(left.shape[0] // 512):
        rows = slice(part * 512, part * 512 + 512)
        basis = left[rows]
        for face in range(2, 6):
            bal, step = face_sum(basis, rhs, face, kc[pair, 0, rows], kc[pair, 1, rows])
            acc[pair, 0, rows] += bal
            acc[pair, 1, rows] += step
        both = jnp.concatenate([acc[pair, 0, rows], acc[pair, 1, rows]], 1)
        high = both.astype(BF)
        low = (both - high.astype(F32)).astype(BF)
        w = right[:, rows]
        one = jnp.dot(w, high, preferred_element_type=F32)
        two = jnp.dot(w[0:88], low, preferred_element_type=F32)
        one = one[0:88] + one[88:176] + two
        total = one if total is None else total + one
    cols = pl.ds(pl.multiple_of(pair * 128, 128), 128)
    res[:, cols] = (total[:, 0:128] - mass[...] * source[:, cols])[0:TERMS]
    jvp[:, cols] = total[0:TERMS, 128:256]


def per_device(
    chaos_modes, newton_heading, source, nodes, weights, k_ref, sensitivity, decay,
    material, neighbors, send_list,
):
    space_count = lax.axis_size("space")
    cells = chaos_modes.shape[1]
    pairs = cells // 128
    halo_depth = send_list.shape[2]
    queue = nodes.shape[0]
    blocks = material.shape[0]
    far = pl.BlockSpec(memory_space=pltpu.HBM)
    vmem = pl.BlockSpec(memory_space=pltpu.VMEM)
    smem = pl.BlockSpec(memory_space=pltpu.SMEM)
    return pl.pallas_call(
        functools.partial(
            whole_kernel, (space_count, lax.axis_size("chaos"), pairs, halo_depth)
        ),
        out_shape=[jax.ShapeDtypeStruct((TERMS, cells), F32)] * 2,
        in_specs=[smem] * 6 + [far] * 5 + [vmem],
        out_specs=[vmem] * 2,
        scratch_shapes=[
            pltpu.VMEM((blocks // 2 + 4, 176, 128), F32),
            pltpu.VMEM((queue, 256), BF),
            pltpu.VMEM((176, queue), BF),
            pltpu.VMEM((88, 1), F32),
            pltpu.VMEM((7, 256, 512), BF),
            pltpu.VMEM((pairs, 2, queue, 128), F32),
            pltpu.VMEM((pairs, 2, queue, 128), F32),
            pltpu.VMEM((TERMS, cells), F32),
            pltpu.VMEM((TERMS, cells), F32),
            pltpu.VMEM((nodes.shape[1], queue), F32),
            pltpu.VMEM((1, queue), F32),
            pltpu.VMEM((8, 256), F32),
            pltpu.VMEM((NMAT, 8, 128), F32),
            pltpu.VMEM((4, 176, 128), F32),
            pltpu.VMEM((4, 176, 128), F32),
            pltpu.SemaphoreType.DMA((16,)),
            pltpu.SemaphoreType.DMA((16,)),
            pltpu.SemaphoreType.DMA((4,)),
            pltpu.SemaphoreType.DMA((4,)),
            pltpu.SemaphoreType.DMA((5,)),
        ],
        compiler_params=pltpu.CompilerParams(
            collective_id=0, has_side_effects=True, vmem_limit_bytes=60 * 1024 * 1024
        ),
    )(
        send_list.reshape(-1), k_ref, sensitivity, decay, material, neighbors.T, chaos_modes,
        newton_heading, nodes.T, weights[None, :], jnp.asarray(order_codes(nodes.shape[1])),
        source[None, :],
    )


def solution(mesh):
    return jax.shard_map(
        per_device,
        mesh=mesh,
        in_specs=(
            P(None, ("space", "chaos")),
            P(None, ("space", "chaos")),
            P(("space", "chaos")),
            P(), P(), P(), P(), P(),
            P("space"),
            P("space", None),
            P("space", None, None),
        ),
        out_specs=(P(None, ("space", "chaos")), P(None, ("space", "chaos"))),
        check_vma=False,
    )
```

profile of v0, /device:TPU:0, one launch (start us, length us, event | category | flops | bytes accessed | tf_op | source)
XLA Modules:
  0.0 51.8 jit_solution(15893238007433441543)
XLA Ops:
  0.6 0.0 copy-start.1
  0.6 0.7 %copy-done.1 = s32[1,8,2]{1,2,0:T(2,128)S(1)} copy-done((s32[1,8,2]{1,2,0:T(2,128)S(1)}, s32[1,8,2]{1,2,0:T(2,128)}, u32[]{:S(2)}) %copy-start.1) | copy-done | bytes 88
  1.3 0.1 copy.15
  1.4 0.6 %reshape.7.picks = s32[16]{0:T(128)} reshape(s32[1,8,2]{2,1,0:T(8,128)S(1)} %copy.15) | data formatting | bytes 128 | tf_op jit(solution)/shard_map/reshape | solution.py:462
  2.0 47.3 %shard_map.131 = (f32[84,1024]{1,0:T(8,128)}, f32[84,1024]{1,0:T(8,128)}) custom-call(s32[16]{0:T(128)} %reshape.7.picks, f32[4]{0:T(128)} %k_ref.1, f32[4,6]{1,0:T(4,128)} %sensitivity.1, f32[4]{0:T(128)} %decay.1, s32[64]{0:T(128)} %material.1, s32[4,64]{1,0:T(4,128)} %bitcast.6, f32[84,1024]{1,0:T(8,128)} %modes_far.1, f32[84,1024]{1,0:T(8,128)} %heading_far.1, ...), custom_call_target="tpu_custom_call" | custom-call | tf_op jit(solution)/shard_map/pallas_call | solution.py:429
  49.2 0.0 copy-start
  49.3 1.8 %copy.18 = f32[84,1024]{1,0:T(8,128)} copy(f32[84,1024]{1,0:T(8,128)} %get-tuple-element.4) | data formatting | bytes 688128
  51.0 0.0 copy-done
  51.1 0.7 %copy.19 = f32[84,1024]{1,0:T(8,128)} copy(f32[84,1024]{1,0:T(8,128)S(1)} %copy-done) | data formatting | bytes 688128
Async XLA Ops:
  0.6 0.7 %copy-start.1 = (s32[1,8,2]{1,2,0:T(2,128)S(1)}, s32[1,8,2]{1,2,0:T(2,128)}, u32[]{:S(2)}) copy-start(s32[1,8,2]{1,2,0:T(2,128)} %param.22) | copy-start | bytes 196
  49.2 1.8 %copy-start = (f32[84,1024]{1,0:T(8,128)S(1)}, f32[84,1024]{1,0:T(8,128)}, u32[]{:S(2)}) copy-start(f32[84,1024]{1,0:T(8,128)} %get-tuple-element.5) | copy-start | bytes 1032196
where the time goes:
time: 52 us; the launch traced here: 51.8 us
  Pallas kernels  47.3 us (91%)
  local copies, waits for them, and re-layouts  3.88 us (7%)
  between operations  0.66 us (1%)
    pallas_call x1, Pallas kernels, per_device(): pl.pallas_call(functools.partial(whole_kernel, (space_count, lax.axis_siz...  47.3 us
    unnamed x7, local copies, waits for them, and re-layouts  3.29 us

commit v1 on v0

v1 whole, which is shorter than its diff:
```python
import functools
import math

import jax
import jax.numpy as jnp
import numpy as np
from jax import lax
from jax.experimental import pallas as pl
from jax.experimental.pallas import tpu as pltpu
from jax.sharding import PartitionSpec as P

NMAT = 4
SITES = 64
TERMS = 84
MAIN = 80
LOG2E = 1.0 / math.log(2.0)
LN2 = math.log(2.0)
OFFSETS = (1, -1, 2, -2)
SPAN = 512
BF = jnp.bfloat16
F32 = jnp.float32


def compositions(remaining, places):
    if places == 1:
        return [[remaining]]
    listing = []
    for leading in range(remaining, -1, -1):
        for trailing in compositions(remaining - leading, places - 1):
            listing.append([leading] + trailing)
    return listing


def chaos_orders(variables):
    listing = []
    for degree in range(4):
        listing = listing + compositions(degree, variables)
    return np.array(listing, dtype=np.int32)


def half_turn(x, wanted):
    return jnp.where(wanted, pltpu.roll(x, 64, 1), x)


def factors(x, o):
    second = (x * x - 1.0) * np.float32(1.0 / math.sqrt(2.0))
    third = (x * x * x - 3.0 * x) * np.float32(1.0 / math.sqrt(6.0))
    return jnp.where(o == 0, 1.0, jnp.where(o == 1, x, jnp.where(o == 2, second, third)))


def order_codes(dims):
    orders = chaos_orders(dims)
    code = (orders * 4 ** np.arange(dims)[None, :]).sum(1)
    out = np.zeros((8, 128), np.float32)
    out[0, :TERMS] = code
    return out


def upright(row):
    return jnp.transpose(jnp.broadcast_to(row, (128, 128)))


def stacked(main, tail, lower):
    row = lax.broadcasted_iota(jnp.int32, tail.shape, 0)
    high = main.astype(BF)
    low = (main - high.astype(F32)).astype(BF)
    tail_high = tail.astype(BF).astype(F32)
    tail_low = tail - tail_high
    if lower:
        parts = [high, high, low]
        ends = [jnp.where(row < 4, tail_high, pltpu.roll(tail_high, 4, 0)), tail_low]
    else:
        parts = [high, low, high]
        ends = [jnp.where(row < 4, tail_high, pltpu.roll(tail_low, 4, 0)), tail_high]
    ends[1] = jnp.where(row < 4, ends[1], 0.0)
    return jnp.concatenate(parts + [jnp.concatenate(ends, 0).astype(BF)], 0)


def fill_tables(nodes_t, weights, codes, left, right, mass):
    dims = nodes_t.shape[0]
    code = upright(codes[0:1, 0:128])[0:88].astype(jnp.int32)
    row = lax.broadcasted_iota(jnp.int32, (88, 1), 0)
    mass[...] = jnp.zeros(mass.shape, F32)

    def body(part, carry):
        span = pl.ds(pl.multiple_of(part * 128, 128), 128)
        value = jnp.ones((88, 128), F32)
        for d in range(dims):
            value = value * factors(nodes_t[d : d + 1, span], (code // 4**d) % 4)
        value = jnp.where(row < TERMS, value, 0.0)
        left[:, span] = stacked(value[0:80], value[80:88], True)
        value = value * weights[:, span]
        mass[...] += jnp.sum(value, axis=1, keepdims=True)
        value = value * 0.25
        high = value.astype(BF).astype(F32)
        right[:, span] = jnp.concatenate([high, value - high], 0).astype(BF)
        return carry

    lax.fori_loop(0, nodes_t.shape[1] // 128, body, 0)


def fill_aux(k_ref, sensitivity, decay, material, table, field):
    row = lax.broadcasted_iota(jnp.int32, (8, 128), 0)
    low_half = lax.broadcasted_iota(jnp.int32, (8, 128), 1) < 64
    dims = sensitivity.shape[1]
    for m in range(NMAT):
        tile = jnp.log(jnp.full((8, 128), k_ref[m], F32))
        for d in range(dims):
            tile = jnp.where(row == d + 1, sensitivity[m, d], tile)
        tile = jnp.where(row == 7, -decay[m], tile) * np.float32(LOG2E)
        table[m, 0] = pltpu.roll(tile, 4, 0)
        table[m, 1] = tile
    for i in range(material.shape[0] // 2):
        a, b = material[2 * i], material[2 * i + 1]
        for f in range(2):
            field[i, f, 84:88] = jnp.where(low_half, table[a, f], table[b, f])[4:8]


def remote(src, dst, send, recv, device):
    return pltpu.make_async_remote_copy(
        src_ref=src, dst_ref=dst, send_sem=send, recv_sem=recv,
        device_id=device, device_id_type=pl.DeviceIdType.MESH,
    )


def greet(space_count, chaos_count, space, chaos):
    barrier = pltpu.get_barrier_semaphore()
    if chaos_count == 4:
        peers = [chaos + 1 - 2 * (chaos % 2), (chaos + 2) % 4]
    else:
        peers = [(chaos + k) % chaos_count for k in range(1, chaos_count)]
    for peer in peers:
        pl.semaphore_signal(
            barrier, inc=1, device_id={"chaos": peer}, device_id_type=pl.DeviceIdType.MESH
        )
    for offset in OFFSETS:
        pl.semaphore_signal(
            barrier, inc=1, device_id={"space": (space + offset + space_count) % space_count},
            device_id_type=pl.DeviceIdType.MESH,
        )
    return barrier, peers


def evaluate(m, h, index, basis, store):
    row = lax.broadcasted_iota(jnp.int32, (8, 128), 0)
    aux = jnp.where(row < 4, pltpu.roll(m[80:88], 4, 0), h[80:88])
    damp = aux[7:8]
    arg = m * damp
    first = arg[0:8] + jnp.where(row < 7, aux, 0.0)
    rate = jnp.transpose(jnp.broadcast_to(damp * np.float32(LN2), (128, 128)))
    sides = [
        jnp.transpose(stacked(x, y, False))
        for x, y in (
            (m[0:80], m[80:88]), (h[0:80], h[80:88]),
            (jnp.concatenate([first, arg[8:80]], 0), arg[80:88]),
        )
    ]
    rows = [s[16 * c : 16 * c + 16] for c in range(8) for s in sides]
    r = jnp.dot(jnp.concatenate(rows, 0), basis, preferred_element_type=F32)
    for c in range(8):
        t = r[48 * c : 48 * c + 16]
        dt = r[48 * c + 16 : 48 * c + 32]
        k = jnp.exp2(r[48 * c + 32 : 48 * c + 48])
        speed = rate[16 * c : 16 * c + 16]
        dk = k * (dt * jnp.concatenate([speed] * (dt.shape[1] // 128), 1))
        block = 2 * index + c // 4
        at = slice(16 * (c % 4), 16 * (c % 4) + 16)
        store[block, 0, at] = t
        store[block, 1, at] = dt
        store[block, 2, at] = k
        store[block, 3, at] = dk


def columns(block, index, store, acc):
    width = 128
    shape = (SITES, width)
    row = lax.broadcasted_iota(jnp.int32, shape, 0)
    top = row == SITES - 1
    bottom = row == 0
    for part in range(store.shape[3] // width):
        at = slice(part * width, part * width + width)
        t, dt, k, dk = [store[block, f, :, at] for f in range(4)]
        up = [pltpu.roll(x, SITES - 1, 0) for x in (t, dt, k, dk)]
        gap = jnp.where(top, 0.0, t - up[0])
        step = jnp.where(top, 0.0, dt - up[1])
        both = k + up[2]
        change = dk + up[3]
        flow = both * gap
        turn = change * gap + both * step
        below = jnp.where(bottom, -4.0 * k * t, pltpu.roll(flow, 1, 0))
        under = jnp.where(bottom, -4.0 * (k * dt + dk * t), pltpu.roll(turn, 1, 0))
        acc[index, 0, :, at] = 2.0 * (flow - below)
        acc[index, 1, :, at] = 2.0 * (turn - under)


def send_halo(space_count, space, picks, field, out, inbox, send, recv):
    low_half = lax.broadcasted_iota(jnp.int32, (1, 128), 1) < 64
    copies = []
    for i, offset in enumerate(OFFSETS):
        target = (space + offset + space_count) % space_count
        e0 = picks[2 * target]
        e1 = picks[2 * target + 1]
        for f in range(2):
            x0 = half_turn(field[e0 // 2, f], e0 % 2 == 1)
            x1 = half_turn(field[e1 // 2, f], e1 % 2 == 0)
            out[i, f] = jnp.where(low_half, x0, x1)
        copy = remote(out.at[i], inbox.at[i], send.at[i], recv.at[i], {"space": target})
        copy.start()
        copies.append(copy)
    return copies


def slot(neighbors, own, block, face, ranks, halo_depth):
    space, space_count, blocks = ranks
    entry = neighbors[face, block]
    away = jnp.maximum(entry - blocks, 0)
    distance = (space - away // halo_depth + space_count) % space_count
    order = jnp.where(
        distance == 1, 0, jnp.where(distance == space_count - 1, 1, jnp.where(distance == 2, 2, 3))
    )
    index = jnp.where(
        entry >= blocks, blocks + order * halo_depth + away % halo_depth, entry
    )
    return jnp.where(entry >= 0, index, own)


def faces(pair, base, ranks, halo_depth, neighbors, store, acc, bal):
    for j in range(2):
        own = 2 * (base + pair) + j
        mine = 2 * pair + j
        others = [slot(neighbors, own, own, f, ranks, halo_depth) for f in range(4)]
        for c in range(SITES // 16):
            rows = slice(16 * c, 16 * c + 16)
            for part in range(store.shape[3] // 256):
                at = slice(part * 256, part * 256 + 256)
                t, dt, k, dk = [store[own, f, rows, at] for f in range(4)]
                flow = acc[mine, 0, rows, at]
                turn = acc[mine, 1, rows, at]
                for e in others:
                    gap = t - store[e, 0, rows, at]
                    step = dt - store[e, 1, rows, at]
                    both = k + store[e, 2, rows, at]
                    change = dk + store[e, 3, rows, at]
                    flow += both * gap
                    turn += change * gap + both * step
                for side, x in ((0, flow), (1, turn)):
                    high = x.astype(BF)
                    spot = slice(128 * side + 64 * j + 16 * c, 128 * side + 64 * j + 16 * c + 16)
                    bal[0, spot, at] = high
                    bal[1, spot, at] = (x - high.astype(F32)).astype(BF)


def project(pair, nodes_at, first, right, bal, mass, source, res, jvp):
    turned = (((1,), (1,)), ((), ()))
    one = lax.dot_general(right[:, nodes_at], bal[0], turned, preferred_element_type=F32)
    two = lax.dot_general(right[0:88, nodes_at], bal[1], turned, preferred_element_type=F32)
    total = one[0:88] + one[88:176] + two
    cols = pl.ds(pl.multiple_of(pair * 128, 128), 128)
    if first:
        res[:, cols] = (total[:, 0:128] - mass[...] * source[:, cols])[0:TERMS]
        jvp[:, cols] = total[0:TERMS, 128:256]
    else:
        res[:, cols] += total[0:TERMS, 0:128]
        jvp[:, cols] += total[0:TERMS, 128:256]


def whole_kernel(
    sizes, picks, k_ref, sensitivity, decay, material, neighbors, modes_far, heading_far,
    nodes_far, weights_far, codes_far, source, res, jvp,
    field, left, right, mass, store, acc, bal,
    nodes_t, weights, codes, table, out, inbox,
    send, recv, halo_send, halo_recv, near, local,
):
    space_count, chaos_count, pairs, halo_depth = sizes
    space = lax.axis_index("space")
    chaos = lax.axis_index("chaos")
    blocks = material.shape[0]
    base = chaos * pairs
    ranks = (space, space_count, blocks)
    barrier, peers = greet(space_count, chaos_count, space, chaos)
    loads = [
        pltpu.make_async_copy(
            far.at[:, i * 128 : i * 128 + 128], field.at[base + i, f, 0:TERMS],
            local.at[2 * i + f],
        )
        for i in range(pairs)
        for f, far in enumerate((modes_far, heading_far))
    ]
    extras = [
        pltpu.make_async_copy(a, b, near.at[i])
        for i, (a, b) in enumerate(
            [(nodes_far, nodes_t), (weights_far, weights), (codes_far, codes)]
        )
    ]
    for load in loads + extras:
        load.start()
    for load in loads:
        load.wait()
    pl.semaphore_wait(barrier, len(peers) + len(OFFSETS))

    def block(owner, first, count):
        return field.at[pl.ds(owner * pairs + first, count), :, 0:TERMS]

    def passing(i, owner, first, count, target):
        ref = block(owner, first, count)
        return remote(ref, ref, send.at[i], recv.at[i], {"chaos": target})

    width = store.shape[3]

    def evaluate_span(start, count, nodes_at=slice(0, width)):
        def body(i, carry):
            evaluate(
                field[start + i, 0], field[start + i, 1], start + i, left[:, nodes_at], store
            )
            return carry

        lax.fori_loop(0, count, body, 0)

    def own_columns():
        def body(i, carry):
            columns(2 * base + i, i, store, acc)
            return carry

        lax.fori_loop(0, 2 * pairs, body, 0)

    def finish(nodes_at, first):
        def late(pair, carry):
            faces(pair, base, ranks, halo_depth, neighbors, store, acc, bal)
            project(pair, nodes_at, first, right, bal, mass, source, res, jvp)
            return carry

        lax.fori_loop(0, pairs, late, 0)

    def mine():
        fill_aux(k_ref, sensitivity, decay, material, table, field)
        for load in extras:
            load.wait()
        fill_tables(nodes_t, weights, codes, left, right, mass)
        evaluate_span(base, pairs)
        own_columns()

    if chaos_count == 4:
        across, along = peers
        half = pairs // 2
        diagonal = 3 - chaos
        copies = [
            passing(0, chaos, 0, half, across), passing(1, chaos, half, half, along),
            passing(2, chaos, half, half, across), passing(3, chaos, 0, half, along),
        ]
        for copy in copies:
            copy.start()
        mine()
        copies[0].wait_recv()
        on = passing(4, across, 0, half, along)
        on.start()
        copies[1].wait_recv()
        over = passing(5, along, half, half, across)
        over.start()
        evaluate_span(across * pairs, half)
        evaluate_span(along * pairs + half, half)
        copies[2].wait_recv()
        evaluate_span(across * pairs + half, half)
        copies[3].wait_recv()
        evaluate_span(along * pairs, half)
        on.wait_recv()
        over.wait_recv()
        copies = copies + [on, over]
        halo = send_halo(space_count, space, picks, field, out, inbox, halo_send, halo_recv)
        evaluate_span(diagonal * pairs, pairs)
    else:
        copies = [passing(i, chaos, 0, pairs, t) for i, t in enumerate(peers)]
        for copy in copies:
            copy.start()
        mine()
        for i, copy in enumerate(copies):
            copy.wait_recv()
        halo = send_halo(space_count, space, picks, field, out, inbox, halo_send, halo_recv)
        for i in range(1, chaos_count):
            evaluate_span(((chaos + i) % chaos_count) * pairs, pairs)
    for i, copy in enumerate(halo):
        copy.wait_recv()
        evaluate(inbox[i, 0], inbox[i, 1], blocks // 2 + i, left[:, 0:width], store)
    finish(slice(0, width), True)

    def again(part, carry):
        nodes_at = pl.ds(pl.multiple_of(part * width, width), width)
        evaluate_span(0, blocks // 2, nodes_at)
        for i in range(len(OFFSETS)):
            evaluate(inbox[i, 0], inbox[i, 1], blocks // 2 + i, left[:, nodes_at], store)
        own_columns()
        finish(nodes_at, False)
        return carry

    if left.shape[1] > width:
        lax.fori_loop(1, left.shape[1] // width, again, 0)
    for copy in copies + halo:
        copy.wait_send()


def per_device(
    chaos_modes, newton_heading, source, nodes, weights, k_ref, sensitivity, decay,
    material, neighbors, send_list,
):
    space_count = lax.axis_size("space")
    cells = chaos_modes.shape[1]
    pairs = cells // 128
    halo_depth = send_list.shape[2]
    queue = nodes.shape[0]
    span = min(queue, SPAN)
    blocks = material.shape[0]
    far = pl.BlockSpec(memory_space=pltpu.HBM)
    vmem = pl.BlockSpec(memory_space=pltpu.VMEM)
    smem = pl.BlockSpec(memory_space=pltpu.SMEM)
    return pl.pallas_call(
        functools.partial(
            whole_kernel, (space_count, lax.axis_size("chaos"), pairs, halo_depth)
        ),
        out_shape=[jax.ShapeDtypeStruct((TERMS, cells), F32)] * 2,
        in_specs=[smem] * 6 + [far] * 5 + [vmem],
        out_specs=[vmem] * 2,
        scratch_shapes=[
            pltpu.VMEM((blocks // 2, 2, 88, 128), F32),
            pltpu.VMEM((256, queue), BF),
            pltpu.VMEM((176, queue), BF),
            pltpu.VMEM((88, 1), F32),
            pltpu.VMEM((blocks + 8, 4, SITES, span), F32),
            pltpu.VMEM((2 * pairs, 2, SITES, span), F32),
            pltpu.VMEM((2, 256, span), BF),
            pltpu.VMEM((nodes.shape[1], queue), F32),
            pltpu.VMEM((1, queue), F32),
            pltpu.VMEM((8, 128), F32),
            pltpu.VMEM((NMAT, 2, 8, 128), F32),
            pltpu.VMEM((4, 2, 88, 128), F32),
            pltpu.VMEM((4, 2, 88, 128), F32),
            pltpu.SemaphoreType.DMA((16,)),
            pltpu.SemaphoreType.DMA((16,)),
            pltpu.SemaphoreType.DMA((4,)),
            pltpu.SemaphoreType.DMA((4,)),
            pltpu.SemaphoreType.DMA((3,)),
            pltpu.SemaphoreType.DMA((2 * pairs,)),
        ],
        compiler_params=pltpu.CompilerParams(
            collective_id=0, has_side_effects=True, vmem_limit_bytes=60 * 1024 * 1024
        ),
    )(
        send_list.reshape(-1), k_ref, sensitivity, decay, material, neighbors.T, chaos_modes,
        newton_heading, nodes.T, weights[None, :], jnp.asarray(order_codes(nodes.shape[1])),
        source[None, :],
    )


def solution(mesh):
    return jax.shard_map(
        per_device,
        mesh=mesh,
        in_specs=(
            P(None, ("space", "chaos")),
            P(None, ("space", "chaos")),
            P(("space", "chaos")),
            P(), P(), P(), P(), P(),
            P("space"),
            P("space", None),
            P("space", None, None),
        ),
        out_specs=(P(None, ("space", "chaos")), P(None, ("space", "chaos"))),
        check_vma=False,
    )
```

time: 52 us -> 49.6 us (0.954)
  Pallas kernels: 47.3 us -> 44.8 us
    pallas_call x1, Pallas kernels: 47.3 us -> 44.8 us  [per_device(): pl.pallas_call(functools.partial(whole_kernel, (space_count, lax.axis_siz...]
where the time goes in v1:
time: 49.6 us; the launch traced here: 49.4 us
  Pallas kernels  44.8 us (90%)
  local copies, waits for them, and re-layouts  3.88 us (8%)
  between operations  0.66 us (1%)
    pallas_call x1, Pallas kernels, per_device(): pl.pallas_call(functools.partial(whole_kernel, (space_count, lax.axis_siz...  44.8 us
    unnamed x7, local copies, waits for them, and re-layouts  3.29 us

profile of v1, /device:TPU:0, one launch (start us, length us, event | category | flops | bytes accessed | tf_op | source)
XLA Modules:
  0.0 49.4 jit_solution(1124870620435203243)
XLA Ops:
  0.6 0.0 copy-start.1
  0.6 0.7 %copy-done.1 = s32[1,8,2]{1,2,0:T(2,128)S(1)} copy-done((s32[1,8,2]{1,2,0:T(2,128)S(1)}, s32[1,8,2]{1,2,0:T(2,128)}, u32[]{:S(2)}) %copy-start.1) | copy-done | bytes 88
  1.3 0.1 copy.15
  1.4 0.6 %reshape.7.picks = s32[16]{0:T(128)} reshape(s32[1,8,2]{2,1,0:T(8,128)S(1)} %copy.15) | data formatting | bytes 128 | tf_op jit(solution)/shard_map/reshape | solution.py:446
  2.0 44.8 %shard_map.131 = (f32[84,1024]{1,0:T(8,128)}, f32[84,1024]{1,0:T(8,128)}) custom-call(s32[16]{0:T(128)} %reshape.7.picks, f32[4]{0:T(128)} %k_ref.1, f32[4,6]{1,0:T(4,128)} %sensitivity.1, f32[4]{0:T(128)} %decay.1, s32[64]{0:T(128)} %material.1, s32[4,64]{1,0:T(4,128)} %bitcast.6, f32[84,1024]{1,0:T(8,128)} %modes_far.1, f32[84,1024]{1,0:T(8,128)} %heading_far.1, ...), custom_call_target="tpu_custom_call" | custom-call | tf_op jit(solution)/shard_map/pallas_call | solution.py:414
  46.8 0.0 copy-start
  46.8 1.8 %copy.18 = f32[84,1024]{1,0:T(8,128)} copy(f32[84,1024]{1,0:T(8,128)} %get-tuple-element.4) | data formatting | bytes 688128
  48.6 0.0 copy-done
  48.6 0.7 %copy.19 = f32[84,1024]{1,0:T(8,128)} copy(f32[84,1024]{1,0:T(8,128)S(1)} %copy-done) | data formatting | bytes 688128
Async XLA Ops:
  0.6 0.7 %copy-start.1 = (s32[1,8,2]{1,2,0:T(2,128)S(1)}, s32[1,8,2]{1,2,0:T(2,128)}, u32[]{:S(2)}) copy-start(s32[1,8,2]{1,2,0:T(2,128)} %param.22) | copy-start | bytes 196
  46.8 1.8 %copy-start = (f32[84,1024]{1,0:T(8,128)S(1)}, f32[84,1024]{1,0:T(8,128)}, u32[]{:S(2)}) copy-start(f32[84,1024]{1,0:T(8,128)} %get-tuple-element.5) | copy-start | bytes 1032196

commit v2 on v1

--- a/solution.py
+++ b/solution.py
@@ -125,10 +125,7 @@
 
 def greet(space_count, chaos_count, space, chaos):
     barrier = pltpu.get_barrier_semaphore()
-    if chaos_count == 4:
-        peers = [chaos + 1 - 2 * (chaos % 2), (chaos + 2) % 4]
-    else:
-        peers = [(chaos + k) % chaos_count for k in range(1, chaos_count)]
+    peers = [(chaos + k) % chaos_count for k in range(1, chaos_count)]
     for peer in peers:
         pl.semaphore_signal(
             barrier, inc=1, device_id={"chaos": peer}, device_id_type=pl.DeviceIdType.MESH
@@ -193,17 +190,19 @@
         acc[index, 1, :, at] = 2.0 * (turn - under)
 
 
+def pack_halo(e0, e1, field, out):
+    low_half = lax.broadcasted_iota(jnp.int32, (1, 128), 1) < 64
+    for f in range(2):
+        x0 = half_turn(field[e0 // 2, f], e0 % 2 == 1)
+        x1 = half_turn(field[e1 // 2, f], e1 % 2 == 0)
+        out[f] = jnp.where(low_half, x0, x1)
+
+
 def send_halo(space_count, space, picks, field, out, inbox, send, recv):
-    low_half = lax.broadcasted_iota(jnp.int32, (1, 128), 1) < 64
     copies = []
     for i, offset in enumerate(OFFSETS):
         target = (space + offset + space_count) % space_count
-        e0 = picks[2 * target]
-        e1 = picks[2 * target + 1]
-        for f in range(2):
-            x0 = half_turn(field[e0 // 2, f], e0 % 2 == 1)
-            x1 = half_turn(field[e1 // 2, f], e1 % 2 == 0)
-            out[i, f] = jnp.where(low_half, x0, x1)
+        pack_halo(picks[0, target], picks[1, target], field, out.at[i])
         copy = remote(out.at[i], inbox.at[i], send.at[i], recv.at[i], {"space": target})
         copy.start()
         copies.append(copy)
@@ -224,15 +223,15 @@
     return jnp.where(entry >= 0, index, own)
 
 
-def faces(pair, base, ranks, halo_depth, neighbors, store, acc, bal):
+def faces(pair, local, ranks, halo_depth, neighbors, store, acc, bal):
     for j in range(2):
-        own = 2 * (base + pair) + j
-        mine = 2 * pair + j
+        own = 2 * pair + j
+        mine = 2 * local + j
         others = [slot(neighbors, own, own, f, ranks, halo_depth) for f in range(4)]
         for c in range(SITES // 16):
             rows = slice(16 * c, 16 * c + 16)
-            for part in range(store.shape[3] // 256):
-                at = slice(part * 256, part * 256 + 256)
+            for part in range(store.shape[3] // 128):
+                at = slice(part * 128, part * 128 + 128)
                 t, dt, k, dk = [store[own, f, rows, at] for f in range(4)]
                 flow = acc[mine, 0, rows, at]
                 turn = acc[mine, 1, rows, at]
@@ -250,11 +249,14 @@
                     bal[1, spot, at] = (x - high.astype(F32)).astype(BF)
 
 
-def project(pair, nodes_at, first, right, bal, mass, source, res, jvp):
+def project(nodes_at, right, bal):
     turned = (((1,), (1,)), ((), ()))
     one = lax.dot_general(right[:, nodes_at], bal[0], turned, preferred_element_type=F32)
     two = lax.dot_general(right[0:88, nodes_at], bal[1], turned, preferred_element_type=F32)
-    total = one[0:88] + one[88:176] + two
+    return one[0:88] + one[88:176] + two
+
+
+def keep(total, pair, first, mass, source, res, jvp):
     cols = pl.ds(pl.multiple_of(pair * 128, 128), 128)
     if first:
         res[:, cols] = (total[:, 0:128] - mass[...] * source[:, cols])[0:TERMS]
@@ -325,8 +327,8 @@
 
     def finish(nodes_at, first):
         def late(pair, carry):
-            faces(pair, base, ranks, halo_depth, neighbors, store, acc, bal)
-            project(pair, nodes_at, first, right, bal, mass, source, res, jvp)
+            faces(base + pair, pair, ranks, halo_depth, neighbors, store, acc, bal)
+            keep(project(nodes_at, right, bal), pair, first, mass, source, res, jvp)
             return carry
 
         lax.fori_loop(0, pairs, late, 0)
@@ -339,44 +341,15 @@
         evaluate_span(base, pairs)
         own_columns()
 
-    if chaos_count == 4:
-        across, along = peers
-        half = pairs // 2
-        diagonal = 3 - chaos
-        copies = [
-            passing(0, chaos, 0, half, across), passing(1, chaos, half, half, along),
-            passing(2, chaos, half, half, across), passing(3, chaos, 0, half, along),
-        ]
-        for copy in copies:
-            copy.start()
-        mine()
-        copies[0].wait_recv()
-        on = passing(4, across, 0, half, along)
-        on.start()
-        copies[1].wait_recv()
-        over = passing(5, along, half, half, across)
-        over.start()
-        evaluate_span(across * pairs, half)
-        evaluate_span(along * pairs + half, half)
-        copies[2].wait_recv()
-        evaluate_span(across * pairs + half, half)
-        copies[3].wait_recv()
-        evaluate_span(along * pairs, half)
-        on.wait_recv()
-        over.wait_recv()
-        copies = copies + [on, over]
-        halo = send_halo(space_count, space, picks, field, out, inbox, halo_send, halo_recv)
-        evaluate_span(diagonal * pairs, pairs)
-    else:
-        copies = [passing(i, chaos, 0, pairs, t) for i, t in enumerate(peers)]
-        for copy in copies:
-            copy.start()
-        mine()
-        for i, copy in enumerate(copies):
-            copy.wait_recv()
-        halo = send_halo(space_count, space, picks, field, out, inbox, halo_send, halo_recv)
-        for i in range(1, chaos_count):
-            evaluate_span(((chaos + i) % chaos_count) * pairs, pairs)
+    copies = [passing(i, chaos, 0, pairs, t) for i, t in enumerate(peers)]
+    for copy in copies:
+        copy.start()
+    mine()
+    for i, copy in enumerate(copies):
+        copy.wait_recv()
+    halo = send_halo(space_count, space, picks, field, out, inbox, halo_send, halo_recv)
+    for i in range(1, chaos_count):
+        evaluate_span(((chaos + i) % chaos_count) * pairs, pairs)
     for i, copy in enumerate(halo):
         copy.wait_recv()
         evaluate(inbox[i, 0], inbox[i, 1], blocks // 2 + i, left[:, 0:width], store)
@@ -443,15 +416,406 @@
             collective_id=0, has_side_effects=True, vmem_limit_bytes=60 * 1024 * 1024
         ),
     )(
-        send_list.reshape(-1), k_ref, sensitivity, decay, material, neighbors.T, chaos_modes,
+        send_list[0].T, k_ref, sensitivity, decay, material, neighbors.T, chaos_modes,
         newton_heading, nodes.T, weights[None, :], jnp.asarray(order_codes(nodes.shape[1])),
         source[None, :],
     )
 
 
+def paired_kernel(
+    sizes, k_ref, sensitivity, decay, material_far, neighbors_far, picks_far, modes_far,
+    heading_far, nodes_far, weights_far, codes_far, source_far, total,
+    field, mine, left, right, mass, store, acc, bal, stage, source,
+    nodes_t, weights, codes, table, out, inbox, material, neighbors, picks,
+    local, near, first_send, first_recv, on_send, send, recv, halo_send, halo_recv,
+    back_send, back_recv,
+):
+    space_count, pairs, halo_depth = sizes
+    space = lax.axis_index("space")
+    chaos = lax.axis_index("chaos")
+    z, core = space // 2, space % 2
+    y, x = chaos // 2, chaos % 2
+    home = core == x
+    part = 2 * z + x
+    half, piece = pairs // 2, pairs // 4
+    blocks = material.shape[0]
+    ranks = (part, space_count, blocks)
+    rank_x, rank_y, rank_d = 2 * y + 1 - x, 2 - 2 * y + x, 3 - chaos
+
+    def device(index, rank):
+        return {"space": index, "chaos": rank}
+
+    sibling = device(2 * z + 1 - core, chaos)
+
+    def offset(j):
+        return (part + (1 + core) * (1 - 2 * j) + space_count) % space_count
+
+    facing = [device(2 * (offset(j) // 2) + core, 2 * y + offset(j) % 2) for j in range(2)]
+    barrier = pltpu.get_barrier_semaphore()
+    peers = [sibling] + [device(2 * z + k, r) for k in range(2) for r in (rank_x, rank_y)]
+    for peer in peers + facing:
+        pl.semaphore_signal(
+            barrier, inc=1, device_id=peer, device_id_type=pl.DeviceIdType.MESH
+        )
+    loads = [
+        pltpu.make_async_copy(
+            far.at[:, i * 128 : i * 128 + 128], mine.at[i, f], local.at[2 * i + f]
+        )
+        for i in range(pairs)
+        for f, far in enumerate((modes_far, heading_far))
+    ]
+    extras = [
+        pltpu.make_async_copy(a, b, near.at[i])
+        for i, (a, b) in enumerate(
+            [(nodes_far, nodes_t), (weights_far, weights), (codes_far, codes)]
+        )
+    ]
+    for load in loads + extras:
+        load.start()
+    for load in loads:
+        load.wait()
+    pl.semaphore_wait(barrier, len(peers + facing))
+
+    def span(rank, first, count):
+        return field.at[pl.ds(rank * pairs + first, count), :, 0:TERMS]
+
+    firsts = []
+    kind = jnp.where(home, 2, 0)
+    rank_to = jnp.where(home, rank_y, rank_x)
+    for p in range(2):
+        for k in range(2):
+            at = k * half + p * piece
+            i = 2 * p + k
+            firsts.append(
+                remote(
+                    mine.at[at : at + piece], span(chaos, at, piece), first_send.at[i],
+                    recv.at[kind + p], device(2 * z + k, rank_to),
+                )
+            )
+    width = half * 128
+    heat = [source_far.at[:, k * width : k * width + width] for k in range(2)]
+    crossing = [
+        remote(
+            heat[k], source.at[0], first_send.at[4 + k], first_recv.at[5],
+            device(2 * z + k, rank_x),
+        )
+        for k in range(2)
+    ]
+
+    def heat_of(k):
+        return source_far.at[:, pl.ds(pl.multiple_of(k * width, 128), width)]
+
+    tables = ((material_far, material), (neighbors_far, neighbors), (picks_far, picks))
+    given = [
+        remote(a, b, on_send.at[i], first_recv.at[i], sibling)
+        for i, (a, b) in enumerate(tables)
+    ] + [
+        remote(mine, span(chaos, 0, pairs), on_send.at[3], first_recv.at[3], sibling),
+        remote(heat_of(1 - core), source.at[1], on_send.at[4], first_recv.at[4], sibling),
+    ]
+    taken = [
+        pltpu.make_async_copy(a, b, on_send.at[5 + i]) for i, (a, b) in enumerate(tables)
+    ] + [
+        pltpu.make_async_copy(mine, span(chaos, 0, pairs), on_send.at[8]),
+        pltpu.make_async_copy(heat_of(core), source.at[1], on_send.at[9]),
+    ]
+
+    for copy in firsts:
+        copy.start()
+
+    @pl.when(home)
+    def _():
+        for copy in given + taken:
+            copy.start()
+
+    @pl.when(jnp.logical_not(home))
+    def _():
+        for copy in crossing:
+            copy.start()
+
+    for load in extras:
+        load.wait()
+    fill_tables(nodes_t, weights, codes, left, right, mass)
+
+    @pl.when(home)
+    def _():
+        for copy in taken:
+            copy.wait()
+
+    @pl.when(jnp.logical_not(home))
+    def _():
+        for copy in given:
+            copy.wait_recv()
+
+    fill_aux(k_ref, sensitivity, decay, material, table, field)
+
+    def evaluate_span(start, count):
+        def body(i, carry):
+            evaluate(field[start + i, 0], field[start + i, 1], start + i, left[...], store)
+            return carry
+
+        lax.fori_loop(0, count, body, 0)
+
+    def own_columns(rank, at):
+        def body(i, carry):
+            columns(2 * (rank * pairs + core * half) + i, 2 * at + i, store, acc)
+            return carry
+
+        lax.fori_loop(0, 2 * half, body, 0)
+
+    def region(kind, p, side):
+        rank = (rank_x, rank_y, rank_d)[kind]
+        return rank, jnp.where(side == 0, core, 1 - core) * half + p * piece
+
+    later = []
+
+    def arrived(kind, p, side):
+        ref = span(*region(kind, p, side), piece)
+        remote(ref, ref, send.at[0], recv.at[6 * side + 2 * kind + p], sibling).wait_recv()
+        return ref
+
+    def hand_on(ref, kind, p, side, target):
+        copy = remote(
+            ref, ref, send.at[len(later)], recv.at[6 * side + 2 * kind + p], target
+        )
+        copy.start()
+        later.append(copy)
+
+    def take(kind, p):
+        ref = arrived(kind, p, 0)
+        if kind == 0:
+            hand_on(ref, 2, p, 0, device(space, rank_y))
+        hand_on(ref, kind, p, 1, sibling)
+
+    def work(kind, p):
+        for side in range(2):
+            if side == 1:
+                arrived(kind, p, 1)
+            rank, first = region(kind, p, side)
+            evaluate_span(rank * pairs + first, piece)
+
+    evaluate_span(chaos * pairs, pairs)
+    take(0, 0)
+    take(1, 0)
+    work(0, 0)
+    own_columns(chaos, half)
+    take(0, 1)
+    take(1, 1)
+    work(1, 0)
+    work(0, 1)
+    own_columns(rank_x, 0)
+    work(1, 1)
+    take(2, 0)
+    work(2, 0)
+    take(2, 1)
+    arrived(2, 1, 1)
+    halo = []
+    for j in range(2):
+        pack_halo(picks[0, offset(j)], picks[1, offset(j)], field, out.at[j])
+        copy = remote(
+            out.at[j], inbox.at[2 * core + j], halo_send.at[j], halo_recv.at[j], facing[j]
+        )
+        copy.start()
+        halo.append(copy)
+    for side in range(2):
+        rank, first = region(2, 1, side)
+        evaluate_span(rank * pairs + first, piece)
+
+    def halo_pair(i):
+        evaluate(inbox[i, 0], inbox[i, 1], blocks // 2 + i, left[...], store)
+
+    for j in range(2):
+        halo[j].wait_recv()
+        ref = inbox.at[2 * core + j]
+        copy = remote(ref, ref, halo_send.at[2 + j], halo_recv.at[2 + j], sibling)
+        copy.start()
+        later.append(copy)
+    for j in range(2):
+        halo_pair(2 * core + j)
+    for j in range(2):
+        ref = inbox.at[2 - 2 * core + j]
+        remote(ref, ref, halo_send.at[2 + j], halo_recv.at[2 + j], sibling).wait_recv()
+        halo_pair(2 - 2 * core + j)
+
+    def result(i):
+        return stage.at[i, :, 0:TERMS]
+
+    def place(side, i):
+        at = pl.multiple_of((side * half + i) * 128, 128)
+        return total.at[:, :, pl.ds(at, 128)]
+
+    def late(rank, at, i):
+        faces(rank * pairs + core * half + i, at + i, ranks, halo_depth, neighbors, store, acc, bal)
+        sums = project(slice(0, store.shape[3]), right, bal)
+        warm = source[at // half, :, pl.ds(pl.multiple_of(i * 128, 128), 128)]
+        stage[at + i, 0] = sums[:, 0:128] - mass[...] * warm
+        stage[at + i, 1] = sums[:, 128:256]
+
+    def back_across(i):
+        return remote(
+            result(i), place(core, i), back_send.at[i], back_recv.at[core * half + i],
+            device(part, rank_x),
+        )
+
+    def back_beside(i):
+        return remote(
+            result(half + i), place(core, i), back_send.at[half + i],
+            back_recv.at[2 * half + i], sibling,
+        )
+
+    def back_here(i):
+        return pltpu.make_async_copy(
+            result(half + i), place(core, i), back_send.at[half + i]
+        )
+
+    def far_pair(i, carry):
+        late(rank_x, 0, i)
+        back_across(i).start()
+        return carry
+
+    def near_pair(i, carry):
+        late(chaos, half, i)
+
+        @pl.when(home)
+        def _():
+            back_here(i).start()
+
+        @pl.when(jnp.logical_not(home))
+        def _():
+            back_beside(i).start()
+
+        return carry
+
+    remote(heat[0], source.at[0], first_send.at[0], first_recv.at[5], sibling).wait_recv()
+    lax.fori_loop(0, half, far_pair, 0)
+    lax.fori_loop(0, half, near_pair, 0)
+    for copy in firsts + later + halo:
+        copy.wait_send()
+    for i in range(half):
+        back_across(i).wait_send()
+
+    @pl.when(home)
+    def _():
+        for copy in given:
+            copy.wait_send()
+        for i in range(half):
+            back_here(i).wait()
+            remote(
+                result(half + i), place(1 - core, i), back_send.at[half + i],
+                back_recv.at[2 * half + i], sibling,
+            ).wait_recv()
+
+    @pl.when(jnp.logical_not(home))
+    def _():
+        for copy in crossing:
+            copy.wait_send()
+        for i in range(half):
+            back_beside(i).wait_send()
+            for k in range(2):
+                remote(
+                    result(i), place(k, i), back_send.at[i], back_recv.at[k * half + i],
+                    sibling,
+                ).wait_recv()
+
+
+def part_kernel(total, res, jvp, held, into, onto):
+    half = total.shape[2] // 2
+    cuts = [(i, k * half) for i in range(2) for k in range(2)]
+    reads, writes = [], []
+    for j, (i, at) in enumerate(cuts):
+        there = (res, jvp)[i].at[:, at : at + half]
+        reads.append(pltpu.make_async_copy(total.at[i, :, at : at + half], held.at[j], into.at[j]))
+        writes.append(pltpu.make_async_copy(held.at[j], there, onto.at[j]))
+    for copy in reads:
+        copy.start()
+    for read, write in zip(reads, writes):
+        read.wait()
+        write.start()
+    for copy in writes:
+        copy.wait()
+
+
+def parted(total):
+    rows, cells = total.shape[1:]
+    far = pl.BlockSpec(memory_space=pltpu.HBM)
+    return tuple(
+        pl.pallas_call(
+            part_kernel,
+            out_shape=[jax.ShapeDtypeStruct((rows, cells), F32)] * 2,
+            in_specs=[far],
+            out_specs=[far] * 2,
+            scratch_shapes=[
+                pltpu.VMEM((4, rows, cells // 2), F32),
+                pltpu.SemaphoreType.DMA((4,)), pltpu.SemaphoreType.DMA((4,)),
+            ],
+        )(total)
+    )
+
+
+def paired_device(
+    chaos_modes, newton_heading, source, nodes, weights, k_ref, sensitivity, decay,
+    material, neighbors, send_list,
+):
+    space_count = lax.axis_size("space")
+    cells = chaos_modes.shape[1]
+    pairs = cells // 128
+    half = pairs // 2
+    halo_depth = send_list.shape[2]
+    queue = nodes.shape[0]
+    blocks = material.shape[0]
+    far = pl.BlockSpec(memory_space=pltpu.HBM)
+    smem = pl.BlockSpec(memory_space=pltpu.SMEM)
+    dma = pltpu.SemaphoreType.DMA
+    total = pl.pallas_call(
+        functools.partial(paired_kernel, (space_count, pairs, halo_depth)),
+        out_shape=jax.ShapeDtypeStruct((2, TERMS, cells), F32),
+        in_specs=[smem] * 3 + [far] * 9,
+        out_specs=far,
+        scratch_shapes=[
+            pltpu.VMEM((blocks // 2, 2, 88, 128), F32),
+            pltpu.VMEM((pairs, 2, TERMS, 128), F32),
+            pltpu.VMEM((256, queue), BF),
+            pltpu.VMEM((176, queue), BF),
+            pltpu.VMEM((88, 1), F32),
+            pltpu.VMEM((blocks + 8, 4, SITES, queue), F32),
+            pltpu.VMEM((2 * pairs, 2, SITES, queue), F32),
+            pltpu.VMEM((2, 256, queue), BF),
+            pltpu.VMEM((pairs, 2, 88, 128), F32),
+            pltpu.VMEM((2, 1, half * 128), F32),
+            pltpu.VMEM((nodes.shape[1], queue), F32),
+            pltpu.VMEM((1, queue), F32),
+            pltpu.VMEM((8, 128), F32),
+            pltpu.VMEM((NMAT, 2, 8, 128), F32),
+            pltpu.VMEM((2, 2, 88, 128), F32),
+            pltpu.VMEM((4, 2, 88, 128), F32),
+            pltpu.SMEM((blocks,), jnp.int32),
+            pltpu.SMEM((4, blocks), jnp.int32),
+            pltpu.SMEM((halo_depth, space_count), jnp.int32),
+            dma((2 * pairs,)), dma((3,)), dma((6,)), dma((6,)), dma((10,)), dma((8,)),
+            dma((12,)), dma((4,)), dma((4,)), dma((2 * half,)), dma((3 * half,)),
+        ],
+        compiler_params=pltpu.CompilerParams(
+            collective_id=1, has_side_effects=True, vmem_limit_bytes=60 * 1024 * 1024
+        ),
+    )(
+        k_ref, sensitivity, decay, material, neighbors.T, send_list[0].T, chaos_modes,
+        newton_heading, nodes.T, weights[None, :], jnp.asarray(order_codes(nodes.shape[1])),
+        source[None, :],
+    )
+    return parted(total)
+
+
+def device_program(*args):
+    modes, nodes, halo_depth = args[0], args[3], args[10].shape[2]
+    space_count = lax.axis_size("space")
+    paired = lax.axis_size("chaos") == 4 and space_count % 2 == 0 and space_count > 4
+    fits = modes.shape[1] % 512 == 0 and nodes.shape[0] <= SPAN and halo_depth == 2
+    return (paired_device if paired and fits else per_device)(*args)
+
+
 def solution(mesh):
     return jax.shard_map(
-        per_device,
+        device_program,
         mesh=mesh,
         in_specs=(
             P(None, ("space", "chaos")),

time: 49.6 us -> 45.7 us (0.921)
  the two profiles are of different devices: /device:TPU:0 before, /device:TPU:1 now
where the time goes in v2:
time: 45.7 us; the launch traced here: 45.5 us
  Pallas kernels  44.8 us (98%)
  between operations  0.64 us (1%)
    pallas_call x1, Pallas kernels, paired_device(): pl.pallas_call(functools.partial(paired_kernel, (space_count, pairs, halo...  42.9 us
    pallas_call x1, Pallas kernels, parted(): pl.pallas_call(part_kernel, out_shape=[jax.ShapeDtypeStruct((rows, cells)...  1.93 us

profile of v2, /device:TPU:1, one launch (start us, length us, event | category | flops | bytes accessed | tf_op | source)
XLA Modules:
  0.0 45.5 jit_solution(9271460656137959650)
XLA Ops:
  0.6 42.9 %shard_map.131.total = f32[2,84,1024]{2,1,0:T(8,128)} custom-call(f32[4]{0:T(128)} %k_ref.1, f32[4,6]{1,0:T(4,128)} %sensitivity.1, f32[4]{0:T(128)} %decay.1, s32[64]{0:T(128)} %material_far.1, s32[4,64]{1,0:T(4,128)} %bitcast.9, s32[2,8]{1,0:T(2,128)} %bitcast.11, f32[84,1024]{1,0:T(8,128)} %modes_far.1, f32[84,1024]{1,0:T(8,128)} %heading_far.1, ...), custom_call_target="tpu_custom_call" | custom-call | tf_op jit(solution)/shard_map/pallas_call | solution.py:769
  43.5 1.9 %shard_map.132 = (f32[84,1024]{1,0:T(8,128)}, f32[84,1024]{1,0:T(8,128)}) custom-call(f32[2,84,1024]{2,1,0:T(8,128)} %shard_map.131.total), custom_call_target="tpu_custom_call" | custom-call | tf_op jit(solution)/shard_map/pallas_call | solution.py:742

commit v3 on v2

--- a/solution.py
+++ b/solution.py
@@ -423,10 +423,11 @@
 
 
 def paired_kernel(
-    sizes, k_ref, sensitivity, decay, material_far, neighbors_far, picks_far, modes_far,
+    sizes, k_far, sensitivity_far, decay_far, material_far, neighbors_far, picks_far, modes_far,
     heading_far, nodes_far, weights_far, codes_far, source_far, total,
     field, mine, left, right, mass, store, acc, bal, stage, source,
-    nodes_t, weights, codes, table, out, inbox, material, neighbors, picks,
+    nodes_t, weights, codes, table, out, inbox, k_ref, sensitivity, decay, material,
+    neighbors, picks,
     local, near, first_send, first_recv, on_send, send, recv, halo_send, halo_recv,
     back_send, back_recv,
 ):
@@ -467,7 +468,10 @@
     extras = [
         pltpu.make_async_copy(a, b, near.at[i])
         for i, (a, b) in enumerate(
-            [(nodes_far, nodes_t), (weights_far, weights), (codes_far, codes)]
+            [
+                (nodes_far, nodes_t), (weights_far, weights), (codes_far, codes),
+                (k_far, k_ref), (sensitivity_far, sensitivity), (decay_far, decay),
+            ]
         )
     ]
     for load in loads + extras:
@@ -718,40 +722,6 @@
                 ).wait_recv()
 
 
-def part_kernel(total, res, jvp, held, into, onto):
-    half = total.shape[2] // 2
-    cuts = [(i, k * half) for i in range(2) for k in range(2)]
-    reads, writes = [], []
-    for j, (i, at) in enumerate(cuts):
-        there = (res, jvp)[i].at[:, at : at + half]
-        reads.append(pltpu.make_async_copy(total.at[i, :, at : at + half], held.at[j], into.at[j]))
-        writes.append(pltpu.make_async_copy(held.at[j], there, onto.at[j]))
-    for copy in reads:
-        copy.start()
-    for read, write in zip(reads, writes):
-        read.wait()
-        write.start()
-    for copy in writes:
-        copy.wait()
-
-
-def parted(total):
-    rows, cells = total.shape[1:]
-    far = pl.BlockSpec(memory_space=pltpu.HBM)
-    return tuple(
-        pl.pallas_call(
-            part_kernel,
-            out_shape=[jax.ShapeDtypeStruct((rows, cells), F32)] * 2,
-            in_specs=[far],
-            out_specs=[far] * 2,
-            scratch_shapes=[
-                pltpu.VMEM((4, rows, cells // 2), F32),
-                pltpu.SemaphoreType.DMA((4,)), pltpu.SemaphoreType.DMA((4,)),
-            ],
-        )(total)
-    )
-
-
 def paired_device(
     chaos_modes, newton_heading, source, nodes, weights, k_ref, sensitivity, decay,
     material, neighbors, send_list,
@@ -764,13 +734,12 @@
     queue = nodes.shape[0]
     blocks = material.shape[0]
     far = pl.BlockSpec(memory_space=pltpu.HBM)
-    smem = pl.BlockSpec(memory_space=pltpu.SMEM)
     dma = pltpu.SemaphoreType.DMA
     total = pl.pallas_call(
         functools.partial(paired_kernel, (space_count, pairs, halo_depth)),
-        out_shape=jax.ShapeDtypeStruct((2, TERMS, cells), F32),
-        in_specs=[smem] * 3 + [far] * 9,
-        out_specs=far,
+        out_shape=pltpu.VMEM((2, TERMS, cells), F32),
+        in_specs=[far] * 12,
+        out_specs=pl.BlockSpec(memory_space=pltpu.VMEM),
         scratch_shapes=[
             pltpu.VMEM((blocks // 2, 2, 88, 128), F32),
             pltpu.VMEM((pairs, 2, TERMS, 128), F32),
@@ -788,21 +757,24 @@
             pltpu.VMEM((NMAT, 2, 8, 128), F32),
             pltpu.VMEM((2, 2, 88, 128), F32),
             pltpu.VMEM((4, 2, 88, 128), F32),
+            pltpu.SMEM(k_ref.shape, F32),
+            pltpu.SMEM(sensitivity.shape, F32),
+            pltpu.SMEM(decay.shape, F32),
             pltpu.SMEM((blocks,), jnp.int32),
             pltpu.SMEM((4, blocks), jnp.int32),
             pltpu.SMEM((halo_depth, space_count), jnp.int32),
-            dma((2 * pairs,)), dma((3,)), dma((6,)), dma((6,)), dma((10,)), dma((8,)),
+            dma((2 * pairs,)), dma((6,)), dma((6,)), dma((6,)), dma((10,)), dma((8,)),
             dma((12,)), dma((4,)), dma((4,)), dma((2 * half,)), dma((3 * half,)),
         ],
         compiler_params=pltpu.CompilerParams(
-            collective_id=1, has_side_effects=True, vmem_limit_bytes=60 * 1024 * 1024
+            collective_id=1, has_side_effects=True, vmem_limit_bytes=54 * 1024 * 1024
         ),
     )(
         k_ref, sensitivity, decay, material, neighbors.T, send_list[0].T, chaos_modes,
         newton_heading, nodes.T, weights[None, :], jnp.asarray(order_codes(nodes.shape[1])),
         source[None, :],
     )
-    return parted(total)
+    return total[0], total[1]
 
 
 def device_program(*args):

time: 45.7 us -> 43.9 us (0.961)
  Pallas kernels: 44.8 us -> 42.1 us
  local copies, waits for them, and re-layouts: 0 us -> 0.93 us
    pallas_call x1 -> x0, Pallas kernels: 1.93 us -> none  [parted(): pl.pallas_call(part_kernel, out_shape=[jax.ShapeDtypeStruct((rows, cells)...]
    squeeze x0 -> x1, local copies, waits for them, and re-layouts: none -> 0.93 us  [paired_device(): return (total[0], total[1])]
    pallas_call x1, Pallas kernels: 42.9 us -> 42.1 us  [paired_device(): pl.pallas_call(functools.partial(paired_kernel, (space_count, pairs, halo...]
where the time goes in v3:
time: 43.9 us; the launch traced here: 43.7 us
  Pallas kernels  42.1 us (96%)
  local copies, waits for them, and re-layouts  0.93 us (2%)
  between operations  0.64 us (1%)
    pallas_call x1, Pallas kernels, paired_device(): pl.pallas_call(functools.partial(paired_kernel, (space_count, pairs, halo...  42.1 us
    squeeze x1, local copies, waits for them, and re-layouts, paired_device(): return (total[0], total[1])  0.93 us

profile of v3, /device:TPU:1, one launch (start us, length us, event | category | flops | bytes accessed | tf_op | source)
XLA Modules:
  0.0 43.7 jit_solution(3393906147565166319)
XLA Ops:
  0.6 42.1 %shard_map.131 = f32[2,84,1024]{2,1,0:T(8,128)S(1)} custom-call(f32[4]{0:T(128)} %k_far.1, f32[4,6]{1,0:T(4,128)} %sensitivity_far.1, f32[4]{0:T(128)} %decay_far.1, s32[64]{0:T(128)} %material_far.1, s32[4,64]{1,0:T(4,128)} %bitcast.13, s32[2,8]{1,0:T(2,128)} %bitcast.15, f32[84,1024]{1,0:T(8,128)} %modes_far.1, f32[84,1024]{1,0:T(8,128)} %heading_far.1, ...), custom_call_target="tpu_custom_call" | custom-call | tf_op jit(solution)/shard_map/pallas_call | solution.py:738
  42.8 0.9 %slice_bitcast_fusion = (f32[84,1024]{1,0:T(8,128)}, f32[84,1024]{1,0:T(8,128)}) fusion(f32[2,84,1024]{2,1,0:T(8,128)S(1)} %shard_map.131), kind=kLoop, calls=%fused_computation | loop fusion | bytes 1376256 | tf_op jit(solution)/shard_map/squeeze | solution.py:777

commit v4 on v3

--- a/solution.py
+++ b/solution.py
@@ -591,9 +591,9 @@
             hand_on(ref, 2, p, 0, device(space, rank_y))
         hand_on(ref, kind, p, 1, sibling)
 
-    def work(kind, p):
+    def work(kind, p, wait):
         for side in range(2):
-            if side == 1:
+            if side == 1 and wait:
                 arrived(kind, p, 1)
             rank, first = region(kind, p, side)
             evaluate_span(rank * pairs + first, piece)
@@ -601,17 +601,16 @@
     evaluate_span(chaos * pairs, pairs)
     take(0, 0)
     take(1, 0)
-    work(0, 0)
+    work(0, 0, True)
     own_columns(chaos, half)
     take(0, 1)
     take(1, 1)
-    work(1, 0)
-    work(0, 1)
-    own_columns(rank_x, 0)
-    work(1, 1)
+    work(1, 0, True)
+    work(0, 1, True)
+    work(1, 1, True)
     take(2, 0)
-    work(2, 0)
     take(2, 1)
+    arrived(2, 0, 1)
     arrived(2, 1, 1)
     halo = []
     for j in range(2):
@@ -621,9 +620,9 @@
         )
         copy.start()
         halo.append(copy)
-    for side in range(2):
-        rank, first = region(2, 1, side)
-        evaluate_span(rank * pairs + first, piece)
+    work(2, 0, False)
+    work(2, 1, False)
+    own_columns(rank_x, 0)
 
     def halo_pair(i):
         evaluate(inbox[i, 0], inbox[i, 1], blocks // 2 + i, left[...], store)

time: 43.9 us -> 41.9 us (0.954)
  Pallas kernels: 42.1 us -> 40.2 us
    pallas_call x1, Pallas kernels: 42.1 us -> 40.2 us  [paired_device(): pl.pallas_call(functools.partial(paired_kernel, (space_count, pairs, halo...]
where the time goes in v4:
time: 41.9 us; the launch traced here: 41.7 us
  Pallas kernels  40.2 us (96%)
  local copies, waits for them, and re-layouts  0.93 us (2%)
  between operations  0.64 us (2%)
    pallas_call x1, Pallas kernels, paired_device(): pl.pallas_call(functools.partial(paired_kernel, (space_count, pairs, halo...  40.2 us
    squeeze x1, local copies, waits for them, and re-layouts, paired_device(): return (total[0], total[1])  0.93 us

profile of v4, /device:TPU:1, one launch (start us, length us, event | category | flops | bytes accessed | tf_op | source)
XLA Modules:
  0.0 41.7 jit_solution(8136886356752299498)
XLA Ops:
  0.6 40.2 %shard_map.131 = f32[2,84,1024]{2,1,0:T(8,128)S(1)} custom-call(f32[4]{0:T(128)} %k_far.1, f32[4,6]{1,0:T(4,128)} %sensitivity_far.1, f32[4]{0:T(128)} %decay_far.1, s32[64]{0:T(128)} %material_far.1, s32[4,64]{1,0:T(4,128)} %bitcast.13, s32[2,8]{1,0:T(2,128)} %bitcast.15, f32[84,1024]{1,0:T(8,128)} %modes_far.1, f32[84,1024]{1,0:T(8,128)} %heading_far.1, ...), custom_call_target="tpu_custom_call" | custom-call | tf_op jit(solution)/shard_map/pallas_call | solution.py:737
  40.8 0.9 %slice_bitcast_fusion = (f32[84,1024]{1,0:T(8,128)}, f32[84,1024]{1,0:T(8,128)}) fusion(f32[2,84,1024]{2,1,0:T(8,128)S(1)} %shard_map.131), kind=kLoop, calls=%fused_computation | loop fusion | bytes 1376256 | tf_op jit(solution)/shard_map/squeeze | solution.py:776

commit v5 on v4

--- a/solution.py
+++ b/solution.py
@@ -230,8 +230,8 @@
         others = [slot(neighbors, own, own, f, ranks, halo_depth) for f in range(4)]
         for c in range(SITES // 16):
             rows = slice(16 * c, 16 * c + 16)
-            for part in range(store.shape[3] // 128):
-                at = slice(part * 128, part * 128 + 128)
+            for part in range(store.shape[3] // 256):
+                at = slice(part * 256, part * 256 + 256)
                 t, dt, k, dk = [store[own, f, rows, at] for f in range(4)]
                 flow = acc[mine, 0, rows, at]
                 turn = acc[mine, 1, rows, at]
@@ -438,7 +438,9 @@
     y, x = chaos // 2, chaos % 2
     home = core == x
     part = 2 * z + x
-    half, piece = pairs // 2, pairs // 4
+    half = pairs // 2
+    piece = (half - half // 4, half // 4)
+    head = (0, piece[0])
     blocks = material.shape[0]
     ranks = (part, space_count, blocks)
     rank_x, rank_y, rank_d = 2 * y + 1 - x, 2 - 2 * y + x, 3 - chaos
@@ -488,11 +490,11 @@
     rank_to = jnp.where(home, rank_y, rank_x)
     for p in range(2):
         for k in range(2):
-            at = k * half + p * piece
+            at = k * half + head[p]
             i = 2 * p + k
             firsts.append(
                 remote(
-                    mine.at[at : at + piece], span(chaos, at, piece), first_send.at[i],
+                    mine.at[at : at + piece[p]], span(chaos, at, piece[p]), first_send.at[i],
                     recv.at[kind + p], device(2 * z + k, rank_to),
                 )
             )
@@ -569,12 +571,12 @@
 
     def region(kind, p, side):
         rank = (rank_x, rank_y, rank_d)[kind]
-        return rank, jnp.where(side == 0, core, 1 - core) * half + p * piece
+        return rank, jnp.where(side == 0, core, 1 - core) * half + head[p]
 
     later = []
 
     def arrived(kind, p, side):
-        ref = span(*region(kind, p, side), piece)
+        ref = span(*region(kind, p, side), piece[p])
         remote(ref, ref, send.at[0], recv.at[6 * side + 2 * kind + p], sibling).wait_recv()
         return ref
 
@@ -596,7 +598,7 @@
             if side == 1 and wait:
                 arrived(kind, p, 1)
             rank, first = region(kind, p, side)
-            evaluate_span(rank * pairs + first, piece)
+            evaluate_span(rank * pairs + first, piece[p])
 
     evaluate_span(chaos * pairs, pairs)
     take(0, 0)

time: 41.9 us -> 41.3 us (0.986)
  Pallas kernels: 40.2 us -> 39.5 us
    pallas_call x1, Pallas kernels: 40.2 us -> 39.5 us  [paired_device(): pl.pallas_call(functools.partial(paired_kernel, (space_count, pairs, halo...]
where the time goes in v5:
time: 41.3 us; the launch traced here: 41 us
  Pallas kernels  39.5 us (96%)
  local copies, waits for them, and re-layouts  0.93 us (2%)
  between operations  0.64 us (2%)
    pallas_call x1, Pallas kernels, paired_device(): pl.pallas_call(functools.partial(paired_kernel, (space_count, pairs, halo...  39.5 us
    squeeze x1, local copies, waits for them, and re-layouts, paired_device(): return (total[0], total[1])  0.93 us

profile of v5, /device:TPU:1, one launch (start us, length us, event | category | flops | bytes accessed | tf_op | source)
XLA Modules:
  0.0 41.0 jit_solution(79289318211145513)
XLA Ops:
  0.6 39.5 %shard_map.131 = f32[2,84,1024]{2,1,0:T(8,128)S(1)} custom-call(f32[4]{0:T(128)} %k_far.1, f32[4,6]{1,0:T(4,128)} %sensitivity_far.1, f32[4]{0:T(128)} %decay_far.1, s32[64]{0:T(128)} %material_far.1, s32[4,64]{1,0:T(4,128)} %bitcast.13, s32[2,8]{1,0:T(2,128)} %bitcast.15, f32[84,1024]{1,0:T(8,128)} %modes_far.1, f32[84,1024]{1,0:T(8,128)} %heading_far.1, ...), custom_call_target="tpu_custom_call" | custom-call | tf_op jit(solution)/shard_map/pallas_call | solution.py:739
  40.1 0.9 %slice_bitcast_fusion = (f32[84,1024]{1,0:T(8,128)}, f32[84,1024]{1,0:T(8,128)}) fusion(f32[2,84,1024]{2,1,0:T(8,128)S(1)} %shard_map.131), kind=kLoop, calls=%fused_computation | loop fusion | bytes 1376256 | tf_op jit(solution)/shard_map/squeeze | solution.py:778
